TPU v7x, 128 devices: a whole 4x4x4 slice. The times are simulated.
128 devices in a mesh: expert: 16 (over z, x), row: 8 (over y, core).
Axes of the slice: x: 4, y: 4, z: 4, core: 2. Of those that a mesh axis runs over, the one named last changes fastest.
Arguments:
- base_weights: bfloat16 [32, 2, 1536, 4096], P(None, None, 'row', 'expert'), may hold values from -6 to 6
- adapter_up_factor: bfloat16 [32, 2, 64, 1536], P(None, None, None, 'row'), may hold values from -6 to 6
- adapter_down: bfloat16 [32, 2, 64, 4096], P(None, None, 'row', 'expert'), may hold values from -6 to 6
- file_sizes: int32 [16], replicated, may hold values from 1 to 8, 64 in all
- file_writer: int32 [16], replicated, may hold values from 0 to 15, each once
Outputs:
- merged_store: bfloat16 [128, 1536, 4096], P('expert', 'row')
Inputs may be any that keep to these rules, and one draw needn't show every extreme that they name: `file_sizes`: every file holds at least one tensor, together 2 * 32; the largest file holds exactly 8. `file_writer`: each rank along the expert axis owns exactly one file.
All inputs are finite; a program needn't handle non-finite values.
Results may differ from a plain program's by a relative error of at most 0.001.
Values may be sent and summed in bfloat16 or wider, within the bound.
No kernel may reach another device: no remote copies, remote signals or barrier semaphores. Data moves between devices by JAX's collectives and lax.ppermute only.
A program may use at most 192 MiB of HBM per device.

v0:
```python
import jax
import jax.numpy as jnp
from jax import lax
from jax.experimental import pallas as pl
from jax.experimental.pallas import tpu as pltpu
from jax.sharding import PartitionSpec as P

CAP = 8
SIDE = 4
Y = 4
STEP = 8
CAPACITIES = (18, 20, 21, 22, 23, 24, 25, 26, 28, 32)
scaling = 0.125
VMEM = 16 * 1024 * 1024


def lines(first, rows):
    groups = []
    for row in range(rows):
        along_z = (row % 2 == 0) == first
        for at in range(SIDE):
            ranks = [(i * SIDE + at) if along_z else (at * SIDE + i) for i in range(SIDE)]
            groups.append([rank * rows + row for rank in ranks])
    return groups


def send(block, first, k):
    groups = lines(first, lax.axis_size("row"))
    pairs = [(group[i], group[(i + k) % SIDE]) for group in groups for i in range(SIDE)]
    return lax.ppermute(block, ("expert", "row"), pairs)


def route(file_sizes, file_writer, tensors, rank, core):
    files = file_sizes.shape[0]
    ids = jnp.arange(files, dtype=jnp.int32)
    starts = jnp.sum(jnp.where(ids[None, :] < ids[:, None], file_sizes[None, :], 0), axis=1)
    owns = file_writer[None, :] == ids[:, None]
    size_of = jnp.sum(jnp.where(owns, file_sizes[None, :], 0), axis=1)
    wz, wx = ids // SIDE, ids % SIDE
    in_row = (wz[:, None] == wz[None, :]) & (wx[None, :] < wx[:, None])
    in_col = (wx[:, None] == wx[None, :]) & (wz[None, :] < wz[:, None])
    first_row = jnp.sum(jnp.where(in_row, size_of[None, :], 0), axis=1)
    first_col = jnp.sum(jnp.where(in_col, size_of[None, :], 0), axis=1)
    most = jnp.maximum(jnp.max(first_row + size_of), jnp.max(first_col + size_of))
    even = core == 0
    first = jnp.where(even, first_row, first_col)
    f_of, g_of = jnp.where(even, wz, wx), jnp.where(even, wx, wz)

    number = jnp.arange(tensors, dtype=jnp.int32)[:, None]
    inside = (number >= starts[None, :]) & (number < (starts + file_sizes)[None, :])
    first_of_file = jnp.sum(jnp.where(owns, first[:, None], 0), axis=0)
    f_of_file = jnp.sum(jnp.where(owns, f_of[:, None], 0), axis=0)
    mine = ids == rank
    f_here, g_here = jnp.sum(jnp.where(mine, f_of, 0)), jnp.sum(jnp.where(mine, g_of, 0))
    line = jnp.sum(jnp.where(inside, ((f_of_file + SIDE - f_here) % SIDE)[None, :], 0), axis=1)
    spot = jnp.sum(jnp.where(inside, (first_of_file - starts)[None, :] + number, 0), axis=1)
    further = (g_of + SIDE - g_here) % SIDE
    at = (f_of == f_here)[None, :] & (further[None, :] == jnp.arange(SIDE, dtype=jnp.int32)[:, None])
    begin = jnp.sum(jnp.where(at, first[None, :], 0), axis=1)
    size = jnp.sum(jnp.where(at, size_of[None, :], 0), axis=1)
    count = jnp.sum(jnp.where(mine, size_of, 0))
    ints = (jnp.concatenate([line, spot]), jnp.concatenate([begin, size]), jnp.stack([count, core, f_here, g_here]), most)
    return tuple(i.astype(jnp.int32) for i in ints)


def merge_kernel(capacity, place_ref, base_ref, up_ref, down_ref, out_ref, held, sems):
    tensors = held.shape[0]
    steps = tensors // STEP

    def fetch(step):
        part = pl.ds(step * STEP, STEP)
        return pltpu.make_async_copy(base_ref.at[part], held.at[part], sems.at[step])

    for step in range(steps):
        fetch(step).start()

    @pl.loop(0, steps)
    def _(step):
        fetch(step).wait()
        for i in range(STEP):
            tensor = step * STEP + i
            delta = lax.dot_general(
                up_ref[tensor], down_ref[tensor], (((0,), (0,)), ((), ())), preferred_element_type=jnp.float32
            )
            merged = held[tensor].astype(jnp.float32) + scaling * delta
            out_ref[place_ref[tensor] * capacity + place_ref[tensors + tensor]] = merged.astype(jnp.bfloat16)


def merge(place, base, up, down, capacity):
    tensors, rows, cols = base.shape

    def kernel(*refs):
        merge_kernel(capacity, *refs)

    return pl.pallas_call(
        kernel,
        out_shape=jax.ShapeDtypeStruct((SIDE * capacity, rows, cols), jnp.bfloat16),
        in_specs=[
            pl.BlockSpec(memory_space=pltpu.SMEM),
            pl.BlockSpec(memory_space=pl.ANY),
            pl.BlockSpec(memory_space=pltpu.VMEM),
            pl.BlockSpec(memory_space=pltpu.VMEM),
        ],
        out_specs=pl.BlockSpec(memory_space=pltpu.VMEM),
        scratch_shapes=[
            pltpu.VMEM((tensors, rows, cols), jnp.bfloat16),
            pltpu.SemaphoreType.DMA((tensors // STEP,)),
        ],
        compiler_params=pltpu.CompilerParams(vmem_limit_bytes=2 * VMEM),
        name="merge",
    )(place, base, up, down)


def gather(down_here, row):
    tensors, share, cols = down_here.shape
    y, core = row // 2, row % 2
    whole = jnp.zeros((tensors, 2 * Y, share, cols), down_here.dtype)

    def put(whole, part, k, of_core):
        block = (y + Y - k) % Y * 2 + of_core
        return lax.dynamic_update_slice(whole, part[:, None], (0, block, 0, 0))

    around = {0: down_here}
    for k in (1, 3, 2):
        pairs = [(at * 2 + c, (at + k) % Y * 2 + c) for at in range(Y) for c in range(2)]
        around[k] = lax.ppermute(down_here, "row", pairs)
    for k in (0, 1, 3, 2):
        other = lax.ppermute(around[k], "row", [(at, at ^ 1) for at in range(2 * Y)])
        whole = put(put(whole, around[k], k, core), other, k, 1 - core)
    return whole.reshape(tensors, 2 * Y * share, cols)


def regroup_kernel(ks, lists_ref, *refs):
    blocks, outs, sems = refs[: len(ks)], refs[-1 - SIDE : -1], refs[-1]

    def each(act):
        for r in (2, 1, 3, 0):
            begin, size = lists_ref[r], lists_ref[SIDE + r]
            for b, bit in enumerate((8, 4, 2, 1)):

                @pl.when(lax.rem(size, 2 * bit) >= bit)
                def _():
                    before = size - lax.rem(size, 2 * bit)
                    for i, k in enumerate(ks):
                        source = blocks[i].at[pl.ds(begin + before, bit)]
                        act(pltpu.make_async_copy(source, outs[r].at[k, pl.ds(before, bit)], sems.at[b, r, i]))

    each(lambda c: c.start())
    each(lambda c: c.wait())


def regroup(lists, blocks, ks, before):
    rows, cols = blocks[0].shape[1:]

    def kernel(*refs):
        regroup_kernel(ks, *refs)

    operands = [*blocks, *before]
    return pl.pallas_call(
        kernel,
        out_shape=[jax.ShapeDtypeStruct((SIDE, CAP, rows, cols), jnp.bfloat16)] * SIDE,
        grid_spec=pltpu.PrefetchScalarGridSpec(
            num_scalar_prefetch=1,
            grid=(1,),
            in_specs=[pl.BlockSpec(memory_space=pl.ANY)] * len(operands),
            out_specs=[pl.BlockSpec(memory_space=pl.ANY)] * SIDE,
            scratch_shapes=[pltpu.SemaphoreType.DMA((4, SIDE, len(ks)))],
        ),
        input_output_aliases={1 + len(blocks) + i: i for i in range(len(before))},
        compiler_params=pltpu.CompilerParams(vmem_limit_bytes=VMEM),
        cost_estimate=pl.CostEstimate(
            flops=0, bytes_accessed=4 * len(ks) * SIDE * CAP * rows * cols // 2, transcendentals=0
        ),
        name="regroup",
    )(lists, *operands)


def unpack_kernel(rs, clear, meta_ref, *refs):
    blocks, (out_ref, zeros, sems, zero_sems) = refs[: len(rs)], refs[-4:]
    count, core, f_here, g_here = (meta_ref[i] for i in range(4))
    cols = blocks[0].shape[-1]

    def each(act):
        for b, bit in enumerate((8, 4, 2, 1)):

            @pl.when(lax.rem(count, 2 * bit) >= bit)
            def _():
                slots = pl.ds(count - lax.rem(count, 2 * bit), bit)
                for i, r in enumerate(rs):
                    for k in range(SIDE):
                        f, g = lax.rem(f_here + SIDE - k, SIDE), lax.rem(g_here + SIDE - r, SIDE)
                        source = jnp.where(core == 0, f * SIDE + g, g * SIDE + f)
                        at = pl.ds(pl.multiple_of(source * cols, cols), cols)
                        act(pltpu.make_async_copy(blocks[i].at[k, slots], out_ref.at[slots, :, at], sems.at[b, i, k]))

    def dead(act):
        @pl.loop(count, CAP)
        def _(slot):
            act(pltpu.make_async_copy(zeros, out_ref.at[slot], zero_sems.at[slot]))

    each(lambda c: c.start())
    if clear:
        zeros[...] = jnp.zeros_like(zeros)
        dead(lambda c: c.start())
        dead(lambda c: c.wait())
    each(lambda c: c.wait())


def unpack(meta, blocks, rs, before):
    side, slots, rows, cols = blocks[0].shape
    width = side * side * cols

    def kernel(*refs):
        unpack_kernel(rs, not before, *refs)

    return pl.pallas_call(
        kernel,
        out_shape=jax.ShapeDtypeStruct((slots, rows, width), jnp.bfloat16),
        in_specs=[
            pl.BlockSpec(memory_space=pltpu.SMEM),
            *[pl.BlockSpec(memory_space=pltpu.VMEM)] * len(blocks),
            *[pl.BlockSpec(memory_space=pl.ANY)] * len(before),
        ],
        out_specs=pl.BlockSpec(memory_space=pl.ANY),
        scratch_shapes=[
            pltpu.VMEM((rows, width), jnp.bfloat16),
            pltpu.SemaphoreType.DMA((4, len(rs), side)),
            pltpu.SemaphoreType.DMA((slots,)),
        ],
        input_output_aliases={1 + len(blocks): 0} if before else {},
        compiler_params=pltpu.CompilerParams(vmem_limit_bytes=VMEM),
        cost_estimate=pl.CostEstimate(
            flops=0, bytes_accessed=4 * len(rs) * side * slots * rows * cols, transcendentals=0
        ),
        name="unpack",
    )(meta, *blocks, *before)


def to_lines(capacity, place, lists, base, up, down):
    sends = merge(place, base, up, down, capacity)
    far, right, left = (send(sends[k * capacity : (k + 1) * capacity], True, k) for k in (2, 1, 3))
    groups = regroup(lists, [sends, far], (0, 2), [])
    return regroup(lists, [right, left], (1, 3), groups)


def body(base_weights, adapter_up_factor, adapter_down, file_sizes, file_writer):
    tensors = base_weights.shape[0] * base_weights.shape[1]
    base = base_weights.reshape(tensors, *base_weights.shape[2:])
    up = adapter_up_factor.reshape(tensors, *adapter_up_factor.shape[2:])
    down_here = adapter_down.reshape(tensors, *adapter_down.shape[2:])
    place, lists, meta, most = route(
        file_sizes, file_writer, tensors, lax.axis_index("expert"), lax.axis_index("row") % 2
    )
    which = jnp.sum(most > jnp.array(CAPACITIES[:-1], jnp.int32)).astype(jnp.int32)
    down = gather(down_here, lax.axis_index("row"))
    branches = [lambda *a, c=c: to_lines(c, *a) for c in CAPACITIES]
    groups = lax.switch(which, branches, place, lists, base, up, down)
    far, right, left = (send(groups[r], False, r) for r in (2, 1, 3))
    out = unpack(meta, [groups[0], far], (0, 2), [])
    return unpack(meta, [right, left], (1, 3), [out])


def solution(mesh):
    in_specs = (
        P(None, None, "row", "expert"),
        P(None, None, None, "row"),
        P(None, None, "row", "expert"),
        P(),
        P(),
    )
    out_specs = P("expert", "row", None)
    return jax.shard_map(body, mesh=mesh, in_specs=in_specs, out_specs=out_specs, check_vma=False)
```

profile of v0, /device:TPU:0, one launch (start us, length us, event | category | flops | bytes accessed | tf_op | source)
XLA Modules:
  0.0 163.0 jit_solution(5357388351663823464)
XLA Ops:
  0.0 3.3 %collective-permute-start.35 = (bf16[64,8,256]{2,1,0:T(8,128)(2,1)}, bf16[64,8,256]{2,1,0:T(8,128)(2,1)S(1)}, u32[]{:S(2)}, u32[]{:S(2)}) collective-permute-start(bf16[64,8,256]{2,1,0:T(8,128)(2,1)} %bitcast.67), channel_id=1, source_target_pairs={{0,4},{1,5},{2,6},{3,7},{4,0},{5,1},{6,2},{7,3},{8,12},{9,13},{10,... | collective-permute-start | bytes 786440 | tf_op jit(solution)/shard_map/ppermute | solution.py:126
  3.3 1.1 collective-permute-start.33
  4.3 1.0 collective-permute-start.31
  5.3 0.0 collective-permute-start.30
  5.3 0.6 select_reduce_fusion.10
  5.9 0.7 select_reduce_fusion.11
  6.7 0.7 broadcast_compare_fusion
  7.3 0.8 select_reduce_fusion.4
  8.1 0.2 select_reduce_fusion.5
  8.3 0.7 add_reduce_fusion
  10.3 1.3 fusion.2
  11.6 0.7 select_reduce_fusion.3
  12.4 1.2 and_select_fusion
  13.6 0.1 select_reduce_fusion.9
  13.8 0.7 fusion.15
  14.4 0.1 select_reduce_fusion.2
  14.5 0.1 pad_add_fusion.2
  15.3 0.1 pad_add_fusion.1
  15.4 0.0 copy-start
  15.4 0.2 broadcast_in_dim.140
  15.6 1.1 constant_dynamic-update-slice_fusion
  16.8 0.0 collective-permute-done.35
  16.8 0.6 collective-permute-start.36
  17.4 0.0 collective-permute-done.33
  17.4 0.1 collective-permute-start.34
  17.5 0.0 collective-permute-done.31
  17.5 0.4 collective-permute-start.32
  17.9 0.0 collective-permute-done.30
  18.0 1.3 collective-permute-done.32
  19.3 0.0 collective-permute-done.34
  19.4 0.0 collective-permute-done.36
  19.5 0.0 copy-done
  19.5 68.0 %conditional.1 = ((bf16[4,8,192,256]{3,2,1,0:T(8,128)(2,1)}, bf16[4,8,192,256]{3,2,1,0:T(8,128)(2,1)}, bf16[4,8,192,256]{3,2,1,0:T(8,128)(2,1)}, bf16[4,8,192,256]{3,2,1,0:T(8,128)(2,1)})) conditional(s32[]{:T(128)} %clamp.3, (s32[128]{0:T(128)S(1)}, bf16[64,192,256]{2,1,0:T(8,128)(2,1)}, ...), branch_computations={%region_16.17_spmd, %region_17.18_spmd, %region_18.19_spmd, %regio... | conditional | bytes 69206144 | solution.py:257
  19.7 5.0 %merge.16.refs_1_ = bf16[100,192,256]{2,1,0:T(8,128)(2,1)S(1)} custom-call(s32[128]{0:T(128)S(1)} %get-tuple-element.160.refs_0_, bf16[64,192,256]{2,1,0:T(8,128)(2,1)} %get-tuple-element.161.refs_1_, bf16[64,64,192]{2,1,0:T(8,128)(2,1)S(1)} %get-tuple-element.162.refs_2_, bf16[64,64,256]{2,1,0:T(8,128)(2,1)S(1)} %get-tuple-element.163.refs_3_), custom_call_target="tpu_custom_call" | custom-call | tf_op jit(solution)/shard_map/cond/branch_6_fun/merge/pallas_call | solution.py:95
  24.7 0.9 fusion.11
  25.6 4.0 %collective-permute-start.20 = (bf16[25,192,256]{2,1,0:T(8,128)(2,1)S(1)}, bf16[25,192,256]{2,1,0:T(8,128)(2,1)S(1)}, u32[]{:S(2)}, u32[]{:S(2)}) collective-permute-start(bf16[25,192,256]{2,1,0:T(8,128)(2,1)S(1)} %get-tuple-element.234), channel_id=1, source_target_pairs={{0,64},{32,96},{64,0},{96,32},{8,72},{40,104},{72,8},{104,40},{16,... | collective-permute-start | bytes 7372808 | tf_op jit(solution)/shard_map/cond/branch_6_fun/ppermute | solution.py:30
  29.6 0.7 collective-permute-start.19
  30.3 1.3 collective-permute-start.18
  31.6 26.0 %collective-permute-done.20.refs_2_ = bf16[25,192,256]{2,1,0:T(8,128)(2,1)S(1)} collective-permute-done((bf16[25,192,256]{2,1,0:T(8,128)(2,1)S(1)}, bf16[25,192,256]{2,1,0:T(8,128)(2,1)S(1)}, u32[]{:S(2)}, u32[]{:S(2)}) %collective-permute-start.20) | collective-permute-done | bytes 2457632 | tf_op jit(solution)/shard_map/cond/branch_6_fun/ppermute | solution.py:30
  57.6 2.6 %regroup.32 = (bf16[4,8,192,256]{3,2,1,0:T(8,128)(2,1)}, bf16[4,8,192,256]{3,2,1,0:T(8,128)(2,1)}, bf16[4,8,192,256]{3,2,1,0:T(8,128)(2,1)}, bf16[4,8,192,256]{3,2,1,0:T(8,128)(2,1)}) custom-call(s32[8]{0:T(128)S(1)} %get-tuple-element.159.refs_0_, bf16[100,192,256]{2,1,0:T(8,128)(2,1)S(1)} %merge.16.refs_1_, ...), custom_call_target="tpu_custom_call" | custom-call | bytes 6291456 | tf_op jit(solution)/shard_map/cond/branch_6_fun/regroup/pallas_call | solution.py:159
  60.1 24.7 %collective-permute-done.19.refs_2_ = bf16[25,192,256]{2,1,0:T(8,128)(2,1)S(1)} collective-permute-done((bf16[25,192,256]{2,1,0:T(8,128)(2,1)S(1)}, bf16[25,192,256]{2,1,0:T(8,128)(2,1)S(1)}, u32[]{:S(2)}, u32[]{:S(2)}) %collective-permute-start.19) | collective-permute-done | bytes 2457632 | tf_op jit(solution)/shard_map/cond/branch_6_fun/ppermute | solution.py:30
  84.9 0.0 collective-permute-done.18.refs_1_
  84.9 2.6 %regroup.33 = (bf16[4,8,192,256]{3,2,1,0:T(8,128)(2,1)}, bf16[4,8,192,256]{3,2,1,0:T(8,128)(2,1)}, bf16[4,8,192,256]{3,2,1,0:T(8,128)(2,1)}, bf16[4,8,192,256]{3,2,1,0:T(8,128)(2,1)}) custom-call(s32[8]{0:T(128)S(1)} %get-tuple-element.159.refs_0_, ...), custom_call_target="tpu_custom_call", output_to_operand_aliasing={{0}: (3, {}), {1}: (4, {}), {2}: (5, {}), {3}: (6, {})} | custom-call | bytes 6291456 | tf_op jit(solution)/shard_map/cond/branch_6_fun/regroup/pallas_call | solution.py:159
  87.4 3.1 %collective-permute-start.39 = (bf16[4,8,192,256]{3,2,1,0:T(8,128)(2,1)}, bf16[4,8,192,256]{3,2,1,0:T(8,128)(2,1)S(1)}, u32[]{:S(2)}, u32[]{:S(2)}) collective-permute-start(bf16[4,8,192,256]{3,2,1,0:T(8,128)(2,1)} %get-tuple-element.202), channel_id=1, source_target_pairs={{0,16},{8,24},{16,0},{24,8},{32,48},{40,56},{48,32},{56,40},{64,80... | collective-permute-start | bytes 9437192 | tf_op jit(solution)/shard_map/ppermute | solution.py:30
  90.5 0.6 collective-permute-start.37
  91.1 2.7 %collective-permute-start.38 = (bf16[4,8,192,256]{3,2,1,0:T(8,128)(2,1)}, bf16[4,8,192,256]{3,2,1,0:T(8,128)(2,1)S(1)}, u32[]{:S(2)}, u32[]{:S(2)}) collective-permute-start(bf16[4,8,192,256]{3,2,1,0:T(8,128)(2,1)} %get-tuple-element.200), channel_id=1, source_target_pairs={{0,24},{8,0},{16,8},{24,16},{32,56},{40,32},{48,40},{56,48},{64,88... | collective-permute-start | bytes 9437192 | tf_op jit(solution)/shard_map/ppermute | solution.py:30
  93.8 1.9 %pad_add_fusion.refs_0_ = s32[4]{0:T(128)S(1)} fusion(s32[1]{0:T(128)} %bitcast.3, s32[1]{0:T(128)} %bitcast.2, s32[1]{0:T(128)} %bitcast.1, s32[1]{0:T(128)} %bitcast), kind=kLoop, calls=%fused_computation.43 | loop fusion | flops 12 | bytes 32 | tf_op jit(solution)/shard_map/stack | solution.py:62
  95.7 30.9 %collective-permute-done.39.refs_2_ = bf16[4,8,192,256]{3,2,1,0:T(8,128)(2,1)S(1)} collective-permute-done((bf16[4,8,192,256]{3,2,1,0:T(8,128)(2,1)}, bf16[4,8,192,256]{3,2,1,0:T(8,128)(2,1)S(1)}, u32[]{:S(2)}, u32[]{:S(2)}) %collective-permute-start.39) | collective-permute-done | bytes 3145760 | tf_op jit(solution)/shard_map/ppermute | solution.py:30
  126.6 5.9 %unpack.2.refs_3_ = bf16[8,192,4096]{2,1,0:T(8,128)(2,1)} custom-call(s32[4]{0:T(128)S(1)} %pad_add_fusion.refs_0_, bf16[4,8,192,256]{3,2,1,0:T(8,128)(2,1)} %get-tuple-element.201.refs_1_, bf16[4,8,192,256]{3,2,1,0:T(8,128)(2,1)S(1)} %collective-permute-done.39.refs_2_), custom_call_target="tpu_custom_call" | custom-call | bytes 12582912 | tf_op jit(solution)/shard_map/unpack/pallas_call | solution.py:216
  132.6 27.7 %collective-permute-done.37.refs_1_ = bf16[4,8,192,256]{3,2,1,0:T(8,128)(2,1)S(1)} collective-permute-done((bf16[4,8,192,256]{3,2,1,0:T(8,128)(2,1)}, bf16[4,8,192,256]{3,2,1,0:T(8,128)(2,1)S(1)}, u32[]{:S(2)}, u32[]{:S(2)}) %collective-permute-start.37) | collective-permute-done | bytes 3145760 | tf_op jit(solution)/shard_map/ppermute | solution.py:30
  160.2 0.1 collective-permute-done.38.refs_2_
  160.3 2.6 %unpack.3 = bf16[8,192,4096]{2,1,0:T(8,128)(2,1)} custom-call(s32[4]{0:T(128)S(1)} %pad_add_fusion.refs_0_, bf16[4,8,192,256]{3,2,1,0:T(8,128)(2,1)S(1)} %collective-permute-done.37.refs_1_, bf16[4,8,192,256]{3,2,1,0:T(8,128)(2,1)S(1)} %collective-permute-done.38.refs_2_, bf16[8,192,4096]{2,1,0:T(8,128)(2,1)} %unpack.2.refs_3_), custom_call_target="tpu_custom_call", output_to_operand_aliasing={{}: (3, {})} | custom-call | bytes 12582912 | tf_op jit(solution)/shard_map/unpack/pallas_call | solution.py:216
  (10 shorter events, 0.2 us)
Async XLA Ops:
  0.0 16.8 %collective-permute-start.35 = (bf16[64,8,256]{2,1,0:T(8,128)(2,1)}, bf16[64,8,256]{2,1,0:T(8,128)(2,1)S(1)}, u32[]{:S(2)}, u32[]{:S(2)}) collective-permute-start(bf16[64,8,256]{2,1,0:T(8,128)(2,1)} %bitcast.67), channel_id=1, source_target_pairs={{0,4},{1,5},{2,6},{3,7},{4,0},{5,1},{6,2},{7,3},{8,12},{9,13},{10,... | collective-permute-start | bytes 786440 | tf_op jit(solution)/shard_map/ppermute | solution.py:126
  3.3 14.1 %collective-permute-start.33 = (bf16[64,8,256]{2,1,0:T(8,128)(2,1)}, bf16[64,8,256]{2,1,0:T(8,128)(2,1)S(1)}, u32[]{:S(2)}, u32[]{:S(2)}) collective-permute-start(bf16[64,8,256]{2,1,0:T(8,128)(2,1)} %bitcast.68), channel_id=1, source_target_pairs={{0,6},{1,7},{2,0},{3,1},{4,2},{5,3},{6,4},{7,5},{8,14},{9,15},{10,... | collective-permute-start | bytes 786440 | tf_op jit(solution)/shard_map/ppermute | solution.py:126
  4.3 13.1 %collective-permute-start.31 = (bf16[64,8,256]{2,1,0:T(8,128)(2,1)}, bf16[64,8,256]{2,1,0:T(8,128)(2,1)S(1)}, u32[]{:S(2)}, u32[]{:S(2)}) collective-permute-start(bf16[64,8,256]{2,1,0:T(8,128)(2,1)} %bitcast.69), channel_id=1, source_target_pairs={{0,2},{1,3},{2,4},{3,5},{4,6},{5,7},{6,0},{7,1},{8,10},{9,11},{10,... | collective-permute-start | bytes 786440 | tf_op jit(solution)/shard_map/ppermute | solution.py:126
  5.3 12.6 %collective-permute-start.30 = (bf16[64,8,256]{2,1,0:T(8,128)(2,1)}, bf16[64,8,256]{2,1,0:T(8,128)(2,1)S(1)}, u32[]{:S(2)}, u32[]{:S(2)}) collective-permute-start(bf16[64,8,256]{2,1,0:T(8,128)(2,1)} %bitcast.70), channel_id=1, source_target_pairs={{0,1},{1,0},{2,3},{3,2},{4,5},{5,4},{6,7},{7,6},{8,9},{9,8},{10,11... | collective-permute-start | bytes 786440 | tf_op jit(solution)/shard_map/ppermute | solution.py:128
  15.4 4.1 %copy-start = (bf16[32,2,64,192]{3,2,1,0:T(8,128)(2,1)S(1)}, bf16[32,2,64,192]{3,2,1,0:T(8,128)(2,1)}, u32[]{:S(2)}) copy-start(bf16[32,2,64,192]{3,2,1,0:T(8,128)(2,1)} %param.17) | copy-start | bytes 4718596
  16.8 2.7 %collective-permute-start.36 = (bf16[64,8,256]{2,1,0:T(8,128)(2,1)S(1)}, bf16[64,8,256]{2,1,0:T(8,128)(2,1)S(1)}, u32[]{:S(2)}, u32[]{:S(2)}) collective-permute-start(bf16[64,8,256]{2,1,0:T(8,128)(2,1)S(1)} %collective-permute-done.35), channel_id=1, source_target_pairs={{0,1},{1,0},{2,3},{3,2},{4,5},{5,4},{6,7},{7,6},{8,9},{9,8},{10,11... | collective-permute-start | bytes 786440 | tf_op jit(solution)/shard_map/ppermute | solution.py:128
  17.4 2.0 %collective-permute-start.34 = (bf16[64,8,256]{2,1,0:T(8,128)(2,1)S(1)}, bf16[64,8,256]{2,1,0:T(8,128)(2,1)S(1)}, u32[]{:S(2)}, u32[]{:S(2)}) collective-permute-start(bf16[64,8,256]{2,1,0:T(8,128)(2,1)S(1)} %collective-permute-done.33), channel_id=1, source_target_pairs={{0,1},{1,0},{2,3},{3,2},{4,5},{5,4},{6,7},{7,6},{8,9},{9,8},{10,11... | collective-permute-start | bytes 786440 | tf_op jit(solution)/shard_map/ppermute | solution.py:128
  17.5 1.8 %collective-permute-start.32 = (bf16[64,8,256]{2,1,0:T(8,128)(2,1)S(1)}, bf16[64,8,256]{2,1,0:T(8,128)(2,1)S(1)}, u32[]{:S(2)}, u32[]{:S(2)}) collective-permute-start(bf16[64,8,256]{2,1,0:T(8,128)(2,1)S(1)} %collective-permute-done.31), channel_id=1, source_target_pairs={{0,1},{1,0},{2,3},{3,2},{4,5},{5,4},{6,7},{7,6},{8,9},{9,8},{10,11... | collective-permute-start | bytes 786440 | tf_op jit(solution)/shard_map/ppermute | solution.py:128
  25.6 31.9 %collective-permute-start.20 = (bf16[25,192,256]{2,1,0:T(8,128)(2,1)S(1)}, bf16[25,192,256]{2,1,0:T(8,128)(2,1)S(1)}, u32[]{:S(2)}, u32[]{:S(2)}) collective-permute-start(bf16[25,192,256]{2,1,0:T(8,128)(2,1)S(1)} %get-tuple-element.234), channel_id=1, source_target_pairs={{0,64},{32,96},{64,0},{96,32},{8,72},{40,104},{72,8},{104,40},{16,... | collective-permute-start | bytes 7372808 | tf_op jit(solution)/shard_map/cond/branch_6_fun/ppermute | solution.py:30
  29.6 55.3 %collective-permute-start.19 = (bf16[25,192,256]{2,1,0:T(8,128)(2,1)S(1)}, bf16[25,192,256]{2,1,0:T(8,128)(2,1)S(1)}, u32[]{:S(2)}, u32[]{:S(2)}) collective-permute-start(bf16[25,192,256]{2,1,0:T(8,128)(2,1)S(1)} %get-tuple-element.235), channel_id=1, source_target_pairs={{0,96},{32,0},{64,32},{96,64},{8,104},{40,8},{72,40},{104,72},{16,... | collective-permute-start | bytes 7372808 | tf_op jit(solution)/shard_map/cond/branch_6_fun/ppermute | solution.py:30
  30.3 54.6 %collective-permute-start.18 = (bf16[25,192,256]{2,1,0:T(8,128)(2,1)S(1)}, bf16[25,192,256]{2,1,0:T(8,128)(2,1)S(1)}, u32[]{:S(2)}, u32[]{:S(2)}) collective-permute-start(bf16[25,192,256]{2,1,0:T(8,128)(2,1)S(1)} %get-tuple-element.236), channel_id=1, source_target_pairs={{0,32},{32,64},{64,96},{96,0},{8,40},{40,72},{72,104},{104,8},{16,... | collective-permute-start | bytes 7372808 | tf_op jit(solution)/shard_map/cond/branch_6_fun/ppermute | solution.py:30
  87.4 39.2 %collective-permute-start.39 = (bf16[4,8,192,256]{3,2,1,0:T(8,128)(2,1)}, bf16[4,8,192,256]{3,2,1,0:T(8,128)(2,1)S(1)}, u32[]{:S(2)}, u32[]{:S(2)}) collective-permute-start(bf16[4,8,192,256]{3,2,1,0:T(8,128)(2,1)} %get-tuple-element.202), channel_id=1, source_target_pairs={{0,16},{8,24},{16,0},{24,8},{32,48},{40,56},{48,32},{56,40},{64,80... | collective-permute-start | bytes 9437192 | tf_op jit(solution)/shard_map/ppermute | solution.py:30
  90.5 69.7 %collective-permute-start.37 = (bf16[4,8,192,256]{3,2,1,0:T(8,128)(2,1)}, bf16[4,8,192,256]{3,2,1,0:T(8,128)(2,1)S(1)}, u32[]{:S(2)}, u32[]{:S(2)}) collective-permute-start(bf16[4,8,192,256]{3,2,1,0:T(8,128)(2,1)} %get-tuple-element.199), channel_id=1, source_target_pairs={{0,8},{8,16},{16,24},{24,0},{32,40},{40,48},{48,56},{56,32},{64,72... | collective-permute-start | bytes 9437192 | tf_op jit(solution)/shard_map/ppermute | solution.py:30
  91.1 69.2 %collective-permute-start.38 = (bf16[4,8,192,256]{3,2,1,0:T(8,128)(2,1)}, bf16[4,8,192,256]{3,2,1,0:T(8,128)(2,1)S(1)}, u32[]{:S(2)}, u32[]{:S(2)}) collective-permute-start(bf16[4,8,192,256]{3,2,1,0:T(8,128)(2,1)} %get-tuple-element.200), channel_id=1, source_target_pairs={{0,24},{8,0},{16,8},{24,16},{32,56},{40,32},{48,40},{56,48},{64,88... | collective-permute-start | bytes 9437192 | tf_op jit(solution)/shard_map/ppermute | solution.py:30
where the time goes:
time: 165 us; the launch traced here: 163 us
  waiting for transfers between devices  111 us (67%)
  starting transfers between devices  18.7 us (11%)
  Pallas kernels  18.7 us (11%)
  other arithmetic  10 us (6%)
  local copies, waits for them, and re-layouts  2.44 us (1%)
  between operations  2.31 us (1%)
    ppermute x6, waiting for transfers between devices, send(): return lax.ppermute(block, ('expert', 'row'), pairs)  109 us
    ppermute x6, starting transfers between devices, send(): return lax.ppermute(block, ('expert', 'row'), pairs)  12.3 us
    pallas_call x2, Pallas kernels, unpack(): pl.pallas_call(kernel, out_shape=jax.ShapeDtypeStruct((slots, rows, width...  8.5 us
    ppermute x3, starting transfers between devices, gather(): around[k] = lax.ppermute(down_here, 'row', pairs)  5.3 us
    pallas_call x2, Pallas kernels, regroup(): pl.pallas_call(kernel, out_shape=[jax.ShapeDtypeStruct((SIDE, CAP, rows,...  5.13 us
    pallas_call x1, Pallas kernels, merge(): pl.pallas_call(kernel, out_shape=jax.ShapeDtypeStruct((SIDE * capacity, r...  5.02 us
  transfers between devices with their start and end apart: 13, of which 6 were waited for; matrix products, arithmetic and copies ran while one was open for 7% of the time, Pallas kernels for 5%

commit v1 on v0

--- a/solution.py
+++ b/solution.py
@@ -1,5 +1,6 @@
 import jax
 import jax.numpy as jnp
+import numpy as np
 from jax import lax
 from jax.experimental import pallas as pl
 from jax.experimental.pallas import tpu as pltpu
@@ -9,7 +10,7 @@
 SIDE = 4
 Y = 4
 STEP = 8
-CAPACITIES = (18, 20, 21, 22, 23, 24, 25, 26, 28, 32)
+CAPACITIES = (18, 19, 20, 21, 22, 23, 24, 25, 26, 27, 28, 30, 32)
 scaling = 0.125
 VMEM = 16 * 1024 * 1024
 
@@ -32,34 +33,40 @@
 
 def route(file_sizes, file_writer, tensors, rank, core):
     files = file_sizes.shape[0]
-    ids = jnp.arange(files, dtype=jnp.int32)
+    last, shift = SIDE - 1, SIDE.bit_length() - 1
+    ids = np.arange(files, dtype=np.int32)
+    wz, wx = ids // SIDE, ids % SIDE
+    in_row = (wz[:, None] == wz[None, :]) & (wx[None, :] < wx[:, None])
+    in_col = (wx[:, None] == wx[None, :]) & (wz[None, :] < wz[:, None])
     starts = jnp.sum(jnp.where(ids[None, :] < ids[:, None], file_sizes[None, :], 0), axis=1)
     owns = file_writer[None, :] == ids[:, None]
     size_of = jnp.sum(jnp.where(owns, file_sizes[None, :], 0), axis=1)
-    wz, wx = ids // SIDE, ids % SIDE
-    in_row = (wz[:, None] == wz[None, :]) & (wx[None, :] < wx[:, None])
-    in_col = (wx[:, None] == wx[None, :]) & (wz[None, :] < wz[:, None])
     first_row = jnp.sum(jnp.where(in_row, size_of[None, :], 0), axis=1)
     first_col = jnp.sum(jnp.where(in_col, size_of[None, :], 0), axis=1)
     most = jnp.maximum(jnp.max(first_row + size_of), jnp.max(first_col + size_of))
     even = core == 0
     first = jnp.where(even, first_row, first_col)
     f_of, g_of = jnp.where(even, wz, wx), jnp.where(even, wx, wz)
-
-    number = jnp.arange(tensors, dtype=jnp.int32)[:, None]
+    f_here = jnp.where(even, rank >> shift, rank & last)
+    g_here = jnp.where(even, rank & last, rank >> shift)
+
+    number = np.arange(tensors, dtype=np.int32)[:, None]
     inside = (number >= starts[None, :]) & (number < (starts + file_sizes)[None, :])
     first_of_file = jnp.sum(jnp.where(owns, first[:, None], 0), axis=0)
-    f_of_file = jnp.sum(jnp.where(owns, f_of[:, None], 0), axis=0)
-    mine = ids == rank
-    f_here, g_here = jnp.sum(jnp.where(mine, f_of, 0)), jnp.sum(jnp.where(mine, g_of, 0))
-    line = jnp.sum(jnp.where(inside, ((f_of_file + SIDE - f_here) % SIDE)[None, :], 0), axis=1)
+    f_of_file = jnp.where(even, file_writer >> shift, file_writer & last)
+    line = jnp.sum(jnp.where(inside, ((f_of_file + SIDE - f_here) & last)[None, :], 0), axis=1)
     spot = jnp.sum(jnp.where(inside, (first_of_file - starts)[None, :] + number, 0), axis=1)
-    further = (g_of + SIDE - g_here) % SIDE
-    at = (f_of == f_here)[None, :] & (further[None, :] == jnp.arange(SIDE, dtype=jnp.int32)[:, None])
+    further = (g_of + SIDE - g_here) & last
+    at = (f_of == f_here)[None, :] & (further[None, :] == np.arange(SIDE, dtype=np.int32)[:, None])
     begin = jnp.sum(jnp.where(at, first[None, :], 0), axis=1)
     size = jnp.sum(jnp.where(at, size_of[None, :], 0), axis=1)
-    count = jnp.sum(jnp.where(mine, size_of, 0))
-    ints = (jnp.concatenate([line, spot]), jnp.concatenate([begin, size]), jnp.stack([count, core, f_here, g_here]), most)
+    count = jnp.sum(jnp.where(ids == rank, size_of, 0))
+    ints = (
+        jnp.concatenate([line, spot]),
+        jnp.concatenate([begin, size]),
+        jnp.stack([count, core, f_here, g_here]),
+        most,
+    )
     return tuple(i.astype(jnp.int32) for i in ints)
 
 
@@ -113,11 +120,11 @@
 
 def gather(down_here, row):
     tensors, share, cols = down_here.shape
-    y, core = row // 2, row % 2
+    y, core = row >> 1, row & 1
     whole = jnp.zeros((tensors, 2 * Y, share, cols), down_here.dtype)
 
     def put(whole, part, k, of_core):
-        block = (y + Y - k) % Y * 2 + of_core
+        block = ((y + Y - k) & (Y - 1)) * 2 + of_core
         return lax.dynamic_update_slice(whole, part[:, None], (0, block, 0, 0))
 
     around = {0: down_here}
@@ -249,7 +256,7 @@
     up = adapter_up_factor.reshape(tensors, *adapter_up_factor.shape[2:])
     down_here = adapter_down.reshape(tensors, *adapter_down.shape[2:])
     place, lists, meta, most = route(
-        file_sizes, file_writer, tensors, lax.axis_index("expert"), lax.axis_index("row") % 2
+        file_sizes, file_writer, tensors, lax.axis_index("expert"), lax.axis_index("row") & 1
     )
     which = jnp.sum(most > jnp.array(CAPACITIES[:-1], jnp.int32)).astype(jnp.int32)
     down = gather(down_here, lax.axis_index("row"))

time: 165 us -> 151 us (0.915)
  waiting for transfers between devices: 111 us -> 100 us
  other arithmetic: 10 us -> 8.13 us
    ppermute x6, waiting for transfers between devices: 109 us -> 99.1 us  [send(): return lax.ppermute(block, ('expert', 'row'), pairs)]
  transfers between devices with their start and end apart: 13 -> 13, of which waited for: 6 -> 6; matrix products, arithmetic and copies ran while one was open for 7% -> 6% of each run, Pallas kernels for 5% -> 5%
where the time goes in v1:
time: 151 us; the launch traced here: 150 us
  waiting for transfers between devices  100 us (66%)
  starting transfers between devices  18.7 us (12%)
  Pallas kernels  18.3 us (12%)
  other arithmetic  8.13 us (5%)
  between operations  2.26 us (1%)
  local copies, waits for them, and re-layouts  2.2 us (1%)
    ppermute x6, waiting for transfers between devices, send(): return lax.ppermute(block, ('expert', 'row'), pairs)  99.1 us
    ppermute x6, starting transfers between devices, send(): return lax.ppermute(block, ('expert', 'row'), pairs)  12.3 us
    pallas_call x2, Pallas kernels, unpack(): pl.pallas_call(kernel, out_shape=jax.ShapeDtypeStruct((slots, rows, width...  8.52 us
    ppermute x3, starting transfers between devices, gather(): around[k] = lax.ppermute(down_here, 'row', pairs)  5.3 us
    pallas_call x1, Pallas kernels, merge(): pl.pallas_call(kernel, out_shape=jax.ShapeDtypeStruct((SIDE * capacity, r...  5.01 us
    pallas_call x2, Pallas kernels, regroup(): pl.pallas_call(kernel, out_shape=[jax.ShapeDtypeStruct((SIDE, CAP, rows,...  4.76 us
  transfers between devices with their start and end apart: 13, of which 6 were waited for; matrix products, arithmetic and copies ran while one was open for 6% of the time, Pallas kernels for 5%

profile of v1, /device:TPU:0, one launch (start us, length us, event | category | flops | bytes accessed | tf_op | source)
XLA Modules:
  0.0 150.4 jit_solution(10956870352463991325)
XLA Ops:
  0.0 3.3 %collective-permute-start.44 = (bf16[64,8,256]{2,1,0:T(8,128)(2,1)}, bf16[64,8,256]{2,1,0:T(8,128)(2,1)S(1)}, u32[]{:S(2)}, u32[]{:S(2)}) collective-permute-start(bf16[64,8,256]{2,1,0:T(8,128)(2,1)} %bitcast.76), channel_id=1, source_target_pairs={{0,4},{1,5},{2,6},{3,7},{4,0},{5,1},{6,2},{7,3},{8,12},{9,13},{10,... | collective-permute-start | bytes 786440 | tf_op jit(solution)/shard_map/ppermute | solution.py:133
  3.3 1.1 collective-permute-start.42
  4.3 1.0 collective-permute-start.40
  5.3 0.0 collective-permute-start.39
  5.3 0.7 fusion.16
  6.0 0.7 fusion.10
  6.6 0.8 select_reduce_fusion.1
  7.4 0.8 select_reduce_fusion.2
  8.3 1.4 add_reduce_fusion
  9.7 0.7 fusion.5
  11.7 1.3 fusion.15
  13.0 0.1 select_reduce_fusion.5
  13.1 0.7 fusion.30
  13.8 0.1 select_reduce_fusion
  13.9 0.1 pad_add_fusion.2
  14.6 0.1 pad_add_fusion.1
  14.7 0.0 copy-start
  14.7 0.2 broadcast_in_dim.121
  14.9 1.1 constant_dynamic-update-slice_fusion
  16.1 0.0 collective-permute-done.44
  16.1 0.6 collective-permute-start.45
  16.7 0.0 collective-permute-done.42
  16.7 0.1 collective-permute-start.43
  16.8 0.0 collective-permute-done.40
  16.8 0.4 collective-permute-start.41
  17.2 0.0 collective-permute-done.39
  17.3 1.3 collective-permute-done.41
  18.6 0.0 collective-permute-done.43
  18.7 0.0 collective-permute-done.45
  18.8 0.0 copy-done
  18.8 54.9 %conditional.1 = ((bf16[4,8,192,256]{3,2,1,0:T(8,128)(2,1)}, bf16[4,8,192,256]{3,2,1,0:T(8,128)(2,1)}, bf16[4,8,192,256]{3,2,1,0:T(8,128)(2,1)}, bf16[4,8,192,256]{3,2,1,0:T(8,128)(2,1)})) conditional(s32[]{:T(128)} %clamp.3, (s32[128]{0:T(128)S(1)}, bf16[64,192,256]{2,1,0:T(8,128)(2,1)}, ...), branch_computations={%region_13.14_spmd, %region_14.15_spmd, %region_15.16_spmd, %regio... | conditional | bytes 69206144 | solution.py:264
  18.8 5.0 %merge.14.refs_1_ = bf16[76,192,256]{2,1,0:T(8,128)(2,1)S(1)} custom-call(s32[128]{0:T(128)S(1)} %get-tuple-element.145.refs_0_, bf16[64,192,256]{2,1,0:T(8,128)(2,1)} %get-tuple-element.146.refs_1_, bf16[64,64,192]{2,1,0:T(8,128)(2,1)S(1)} %get-tuple-element.147.refs_2_, bf16[64,64,256]{2,1,0:T(8,128)(2,1)S(1)} %get-tuple-element.148.refs_3_), custom_call_target="tpu_custom_call" | custom-call | tf_op jit(solution)/shard_map/cond/branch_1_fun/merge/pallas_call | solution.py:102
  23.8 0.7 fusion.18
  24.5 4.0 %collective-permute-start.5 = (bf16[19,192,256]{2,1,0:T(8,128)(2,1)S(1)}, bf16[19,192,256]{2,1,0:T(8,128)(2,1)S(1)}, u32[]{:S(2)}, u32[]{:S(2)}) collective-permute-start(bf16[19,192,256]{2,1,0:T(8,128)(2,1)S(1)} %get-tuple-element.274), channel_id=1, source_target_pairs={{0,64},{32,96},{64,0},{96,32},{8,72},{40,104},{72,8},{104,40},{16,... | collective-permute-start | bytes 5603336 | tf_op jit(solution)/shard_map/cond/branch_1_fun/ppermute | solution.py:31
  28.5 0.7 collective-permute-start.4
  29.2 1.3 collective-permute-start.3
  30.5 19.6 %collective-permute-done.5.refs_2_ = bf16[19,192,256]{2,1,0:T(8,128)(2,1)S(1)} collective-permute-done((bf16[19,192,256]{2,1,0:T(8,128)(2,1)S(1)}, bf16[19,192,256]{2,1,0:T(8,128)(2,1)S(1)}, u32[]{:S(2)}, u32[]{:S(2)}) %collective-permute-start.5) | collective-permute-done | bytes 1867808 | tf_op jit(solution)/shard_map/cond/branch_1_fun/ppermute | solution.py:31
  50.1 2.4 %regroup.28 = (bf16[4,8,192,256]{3,2,1,0:T(8,128)(2,1)}, bf16[4,8,192,256]{3,2,1,0:T(8,128)(2,1)}, bf16[4,8,192,256]{3,2,1,0:T(8,128)(2,1)}, bf16[4,8,192,256]{3,2,1,0:T(8,128)(2,1)}) custom-call(s32[8]{0:T(128)S(1)} %get-tuple-element.144.refs_0_, bf16[76,192,256]{2,1,0:T(8,128)(2,1)S(1)} %merge.14.refs_1_, ...), custom_call_target="tpu_custom_call" | custom-call | bytes 6291456 | tf_op jit(solution)/shard_map/cond/branch_1_fun/regroup/pallas_call | solution.py:166
  52.5 18.6 %collective-permute-done.4.refs_2_ = bf16[19,192,256]{2,1,0:T(8,128)(2,1)S(1)} collective-permute-done((bf16[19,192,256]{2,1,0:T(8,128)(2,1)S(1)}, bf16[19,192,256]{2,1,0:T(8,128)(2,1)S(1)}, u32[]{:S(2)}, u32[]{:S(2)}) %collective-permute-start.4) | collective-permute-done | bytes 1867808 | tf_op jit(solution)/shard_map/cond/branch_1_fun/ppermute | solution.py:31
  71.1 0.0 collective-permute-done.3.refs_1_
  71.1 2.4 %regroup.29 = (bf16[4,8,192,256]{3,2,1,0:T(8,128)(2,1)}, bf16[4,8,192,256]{3,2,1,0:T(8,128)(2,1)}, bf16[4,8,192,256]{3,2,1,0:T(8,128)(2,1)}, bf16[4,8,192,256]{3,2,1,0:T(8,128)(2,1)}) custom-call(s32[8]{0:T(128)S(1)} %get-tuple-element.144.refs_0_, ...), custom_call_target="tpu_custom_call", output_to_operand_aliasing={{0}: (3, {}), {1}: (4, {}), {2}: (5, {}), {3}: (6, {})} | custom-call | bytes 6291456 | tf_op jit(solution)/shard_map/cond/branch_1_fun/regroup/pallas_call | solution.py:166
  73.7 3.1 %collective-permute-start.48 = (bf16[4,8,192,256]{3,2,1,0:T(8,128)(2,1)}, bf16[4,8,192,256]{3,2,1,0:T(8,128)(2,1)S(1)}, u32[]{:S(2)}, u32[]{:S(2)}) collective-permute-start(bf16[4,8,192,256]{3,2,1,0:T(8,128)(2,1)} %get-tuple-element.259), channel_id=1, source_target_pairs={{0,16},{8,24},{16,0},{24,8},{32,48},{40,56},{48,32},{56,40},{64,80... | collective-permute-start | bytes 9437192 | tf_op jit(solution)/shard_map/ppermute | solution.py:31
  76.8 0.6 collective-permute-start.46
  77.4 2.6 %collective-permute-start.47 = (bf16[4,8,192,256]{3,2,1,0:T(8,128)(2,1)}, bf16[4,8,192,256]{3,2,1,0:T(8,128)(2,1)S(1)}, u32[]{:S(2)}, u32[]{:S(2)}) collective-permute-start(bf16[4,8,192,256]{3,2,1,0:T(8,128)(2,1)} %get-tuple-element.257), channel_id=1, source_target_pairs={{0,24},{8,0},{16,8},{24,16},{32,56},{40,32},{48,40},{56,48},{64,88... | collective-permute-start | bytes 9437192 | tf_op jit(solution)/shard_map/ppermute | solution.py:31
  80.0 0.7 pad_add_fusion.refs_0_
  80.7 32.2 %collective-permute-done.48.refs_2_ = bf16[4,8,192,256]{3,2,1,0:T(8,128)(2,1)S(1)} collective-permute-done((bf16[4,8,192,256]{3,2,1,0:T(8,128)(2,1)}, bf16[4,8,192,256]{3,2,1,0:T(8,128)(2,1)S(1)}, u32[]{:S(2)}, u32[]{:S(2)}) %collective-permute-start.48) | collective-permute-done | bytes 3145760 | tf_op jit(solution)/shard_map/ppermute | solution.py:31
  112.9 4.9 %unpack.2.refs_3_ = bf16[8,192,4096]{2,1,0:T(8,128)(2,1)} custom-call(s32[4]{0:T(128)S(1)} %pad_add_fusion.refs_0_, bf16[4,8,192,256]{3,2,1,0:T(8,128)(2,1)} %get-tuple-element.258.refs_1_, bf16[4,8,192,256]{3,2,1,0:T(8,128)(2,1)S(1)} %collective-permute-done.48.refs_2_), custom_call_target="tpu_custom_call" | custom-call | bytes 12582912 | tf_op jit(solution)/shard_map/unpack/pallas_call | solution.py:223
  117.8 28.7 %collective-permute-done.46.refs_1_ = bf16[4,8,192,256]{3,2,1,0:T(8,128)(2,1)S(1)} collective-permute-done((bf16[4,8,192,256]{3,2,1,0:T(8,128)(2,1)}, bf16[4,8,192,256]{3,2,1,0:T(8,128)(2,1)S(1)}, u32[]{:S(2)}, u32[]{:S(2)}) %collective-permute-start.46) | collective-permute-done | bytes 3145760 | tf_op jit(solution)/shard_map/ppermute | solution.py:31
  146.5 0.1 collective-permute-done.47.refs_2_
  146.6 3.6 %unpack.3 = bf16[8,192,4096]{2,1,0:T(8,128)(2,1)} custom-call(s32[4]{0:T(128)S(1)} %pad_add_fusion.refs_0_, bf16[4,8,192,256]{3,2,1,0:T(8,128)(2,1)S(1)} %collective-permute-done.46.refs_1_, bf16[4,8,192,256]{3,2,1,0:T(8,128)(2,1)S(1)} %collective-permute-done.47.refs_2_, bf16[8,192,4096]{2,1,0:T(8,128)(2,1)} %unpack.2.refs_3_), custom_call_target="tpu_custom_call", output_to_operand_aliasing={{}: (3, {})} | custom-call | bytes 12582912 | tf_op jit(solution)/shard_map/unpack/pallas_call | solution.py:223
  (7 shorter events, 0.2 us)
Async XLA Ops:
  0.0 16.1 %collective-permute-start.44 = (bf16[64,8,256]{2,1,0:T(8,128)(2,1)}, bf16[64,8,256]{2,1,0:T(8,128)(2,1)S(1)}, u32[]{:S(2)}, u32[]{:S(2)}) collective-permute-start(bf16[64,8,256]{2,1,0:T(8,128)(2,1)} %bitcast.76), channel_id=1, source_target_pairs={{0,4},{1,5},{2,6},{3,7},{4,0},{5,1},{6,2},{7,3},{8,12},{9,13},{10,... | collective-permute-start | bytes 786440 | tf_op jit(solution)/shard_map/ppermute | solution.py:133
  3.3 13.4 %collective-permute-start.42 = (bf16[64,8,256]{2,1,0:T(8,128)(2,1)}, bf16[64,8,256]{2,1,0:T(8,128)(2,1)S(1)}, u32[]{:S(2)}, u32[]{:S(2)}) collective-permute-start(bf16[64,8,256]{2,1,0:T(8,128)(2,1)} %bitcast.77), channel_id=1, source_target_pairs={{0,6},{1,7},{2,0},{3,1},{4,2},{5,3},{6,4},{7,5},{8,14},{9,15},{10,... | collective-permute-start | bytes 786440 | tf_op jit(solution)/shard_map/ppermute | solution.py:133
  4.3 12.4 %collective-permute-start.40 = (bf16[64,8,256]{2,1,0:T(8,128)(2,1)}, bf16[64,8,256]{2,1,0:T(8,128)(2,1)S(1)}, u32[]{:S(2)}, u32[]{:S(2)}) collective-permute-start(bf16[64,8,256]{2,1,0:T(8,128)(2,1)} %bitcast.78), channel_id=1, source_target_pairs={{0,2},{1,3},{2,4},{3,5},{4,6},{5,7},{6,0},{7,1},{8,10},{9,11},{10,... | collective-permute-start | bytes 786440 | tf_op jit(solution)/shard_map/ppermute | solution.py:133
  5.3 11.9 %collective-permute-start.39 = (bf16[64,8,256]{2,1,0:T(8,128)(2,1)}, bf16[64,8,256]{2,1,0:T(8,128)(2,1)S(1)}, u32[]{:S(2)}, u32[]{:S(2)}) collective-permute-start(bf16[64,8,256]{2,1,0:T(8,128)(2,1)} %bitcast.79), channel_id=1, source_target_pairs={{0,1},{1,0},{2,3},{3,2},{4,5},{5,4},{6,7},{7,6},{8,9},{9,8},{10,11... | collective-permute-start | bytes 786440 | tf_op jit(solution)/shard_map/ppermute | solution.py:135
  14.7 4.1 %copy-start = (bf16[32,2,64,192]{3,2,1,0:T(8,128)(2,1)S(1)}, bf16[32,2,64,192]{3,2,1,0:T(8,128)(2,1)}, u32[]{:S(2)}) copy-start(bf16[32,2,64,192]{3,2,1,0:T(8,128)(2,1)} %param.29) | copy-start | bytes 4718596
  16.1 2.7 %collective-permute-start.45 = (bf16[64,8,256]{2,1,0:T(8,128)(2,1)S(1)}, bf16[64,8,256]{2,1,0:T(8,128)(2,1)S(1)}, u32[]{:S(2)}, u32[]{:S(2)}) collective-permute-start(bf16[64,8,256]{2,1,0:T(8,128)(2,1)S(1)} %collective-permute-done.44), channel_id=1, source_target_pairs={{0,1},{1,0},{2,3},{3,2},{4,5},{5,4},{6,7},{7,6},{8,9},{9,8},{10,11... | collective-permute-start | bytes 786440 | tf_op jit(solution)/shard_map/ppermute | solution.py:135
  16.7 2.0 %collective-permute-start.43 = (bf16[64,8,256]{2,1,0:T(8,128)(2,1)S(1)}, bf16[64,8,256]{2,1,0:T(8,128)(2,1)S(1)}, u32[]{:S(2)}, u32[]{:S(2)}) collective-permute-start(bf16[64,8,256]{2,1,0:T(8,128)(2,1)S(1)} %collective-permute-done.42), channel_id=1, source_target_pairs={{0,1},{1,0},{2,3},{3,2},{4,5},{5,4},{6,7},{7,6},{8,9},{9,8},{10,11... | collective-permute-start | bytes 786440 | tf_op jit(solution)/shard_map/ppermute | solution.py:135
  16.8 1.8 %collective-permute-start.41 = (bf16[64,8,256]{2,1,0:T(8,128)(2,1)S(1)}, bf16[64,8,256]{2,1,0:T(8,128)(2,1)S(1)}, u32[]{:S(2)}, u32[]{:S(2)}) collective-permute-start(bf16[64,8,256]{2,1,0:T(8,128)(2,1)S(1)} %collective-permute-done.40), channel_id=1, source_target_pairs={{0,1},{1,0},{2,3},{3,2},{4,5},{5,4},{6,7},{7,6},{8,9},{9,8},{10,11... | collective-permute-start | bytes 786440 | tf_op jit(solution)/shard_map/ppermute | solution.py:135
  24.5 25.6 %collective-permute-start.5 = (bf16[19,192,256]{2,1,0:T(8,128)(2,1)S(1)}, bf16[19,192,256]{2,1,0:T(8,128)(2,1)S(1)}, u32[]{:S(2)}, u32[]{:S(2)}) collective-permute-start(bf16[19,192,256]{2,1,0:T(8,128)(2,1)S(1)} %get-tuple-element.274), channel_id=1, source_target_pairs={{0,64},{32,96},{64,0},{96,32},{8,72},{40,104},{72,8},{104,40},{16,... | collective-permute-start | bytes 5603336 | tf_op jit(solution)/shard_map/cond/branch_1_fun/ppermute | solution.py:31
  28.5 42.6 %collective-permute-start.4 = (bf16[19,192,256]{2,1,0:T(8,128)(2,1)S(1)}, bf16[19,192,256]{2,1,0:T(8,128)(2,1)S(1)}, u32[]{:S(2)}, u32[]{:S(2)}) collective-permute-start(bf16[19,192,256]{2,1,0:T(8,128)(2,1)S(1)} %get-tuple-element.275), channel_id=1, source_target_pairs={{0,96},{32,0},{64,32},{96,64},{8,104},{40,8},{72,40},{104,72},{16,... | collective-permute-start | bytes 5603336 | tf_op jit(solution)/shard_map/cond/branch_1_fun/ppermute | solution.py:31
  29.2 41.9 %collective-permute-start.3 = (bf16[19,192,256]{2,1,0:T(8,128)(2,1)S(1)}, bf16[19,192,256]{2,1,0:T(8,128)(2,1)S(1)}, u32[]{:S(2)}, u32[]{:S(2)}) collective-permute-start(bf16[19,192,256]{2,1,0:T(8,128)(2,1)S(1)} %get-tuple-element.276), channel_id=1, source_target_pairs={{0,32},{32,64},{64,96},{96,0},{8,40},{40,72},{72,104},{104,8},{16,... | collective-permute-start | bytes 5603336 | tf_op jit(solution)/shard_map/cond/branch_1_fun/ppermute | solution.py:31
  73.7 39.2 %collective-permute-start.48 = (bf16[4,8,192,256]{3,2,1,0:T(8,128)(2,1)}, bf16[4,8,192,256]{3,2,1,0:T(8,128)(2,1)S(1)}, u32[]{:S(2)}, u32[]{:S(2)}) collective-permute-start(bf16[4,8,192,256]{3,2,1,0:T(8,128)(2,1)} %get-tuple-element.259), channel_id=1, source_target_pairs={{0,16},{8,24},{16,0},{24,8},{32,48},{40,56},{48,32},{56,40},{64,80... | collective-permute-start | bytes 9437192 | tf_op jit(solution)/shard_map/ppermute | solution.py:31
  76.8 69.7 %collective-permute-start.46 = (bf16[4,8,192,256]{3,2,1,0:T(8,128)(2,1)}, bf16[4,8,192,256]{3,2,1,0:T(8,128)(2,1)S(1)}, u32[]{:S(2)}, u32[]{:S(2)}) collective-permute-start(bf16[4,8,192,256]{3,2,1,0:T(8,128)(2,1)} %get-tuple-element.256), channel_id=1, source_target_pairs={{0,8},{8,16},{16,24},{24,0},{32,40},{40,48},{48,56},{56,32},{64,72... | collective-permute-start | bytes 9437192 | tf_op jit(solution)/shard_map/ppermute | solution.py:31
  77.4 69.2 %collective-permute-start.47 = (bf16[4,8,192,256]{3,2,1,0:T(8,128)(2,1)}, bf16[4,8,192,256]{3,2,1,0:T(8,128)(2,1)S(1)}, u32[]{:S(2)}, u32[]{:S(2)}) collective-permute-start(bf16[4,8,192,256]{3,2,1,0:T(8,128)(2,1)} %get-tuple-element.257), channel_id=1, source_target_pairs={{0,24},{8,0},{16,8},{24,16},{32,56},{40,32},{48,40},{56,48},{64,88... | collective-permute-start | bytes 9437192 | tf_op jit(solution)/shard_map/ppermute | solution.py:31

commit v2 on v1

--- a/solution.py
+++ b/solution.py
@@ -31,7 +31,7 @@
     return lax.ppermute(block, ("expert", "row"), pairs)
 
 
-def route(file_sizes, file_writer, tensors, rank, core):
+def route(file_sizes, file_writer, sizes_late, writer_late, tensors, rank, core):
     files = file_sizes.shape[0]
     last, shift = SIDE - 1, SIDE.bit_length() - 1
     ids = np.arange(files, dtype=np.int32)
@@ -51,9 +51,9 @@
     g_here = jnp.where(even, rank & last, rank >> shift)
 
     number = np.arange(tensors, dtype=np.int32)[:, None]
-    inside = (number >= starts[None, :]) & (number < (starts + file_sizes)[None, :])
+    inside = (number >= starts[None, :]) & (number < (starts + sizes_late)[None, :])
     first_of_file = jnp.sum(jnp.where(owns, first[:, None], 0), axis=0)
-    f_of_file = jnp.where(even, file_writer >> shift, file_writer & last)
+    f_of_file = jnp.where(even, writer_late >> shift, writer_late & last)
     line = jnp.sum(jnp.where(inside, ((f_of_file + SIDE - f_here) & last)[None, :], 0), axis=1)
     spot = jnp.sum(jnp.where(inside, (first_of_file - starts)[None, :] + number, 0), axis=1)
     further = (g_of + SIDE - g_here) & last
@@ -118,20 +118,24 @@
     )(place, base, up, down)
 
 
-def gather(down_here, row):
-    tensors, share, cols = down_here.shape
-    y, core = row >> 1, row & 1
-    whole = jnp.zeros((tensors, 2 * Y, share, cols), down_here.dtype)
-
-    def put(whole, part, k, of_core):
-        block = ((y + Y - k) & (Y - 1)) * 2 + of_core
-        return lax.dynamic_update_slice(whole, part[:, None], (0, block, 0, 0))
-
+def gather_y(down_here):
     around = {0: down_here}
     for k in (1, 3, 2):
         pairs = [(at * 2 + c, (at + k) % Y * 2 + c) for at in range(Y) for c in range(2)]
         around[k] = lax.ppermute(down_here, "row", pairs)
-    for k in (0, 1, 3, 2):
+    return around
+
+
+def gather_core(around, row):
+    tensors, share, cols = around[0].shape
+    y, core = row >> 1, row & 1
+    whole = jnp.zeros((tensors, 2 * Y, share, cols), around[0].dtype)
+
+    def put(whole, part, k, of_core):
+        block = ((y + Y - k) & (Y - 1)) * 2 + of_core
+        return lax.dynamic_update_slice(whole, part[:, None], (0, block, 0, 0))
+
+    for k in (1, 3, 2, 0):
         other = lax.ppermute(around[k], "row", [(at, at ^ 1) for at in range(2 * Y)])
         whole = put(put(whole, around[k], k, core), other, k, 1 - core)
     return whole.reshape(tensors, 2 * Y * share, cols)
@@ -255,11 +259,12 @@
     base = base_weights.reshape(tensors, *base_weights.shape[2:])
     up = adapter_up_factor.reshape(tensors, *adapter_up_factor.shape[2:])
     down_here = adapter_down.reshape(tensors, *adapter_down.shape[2:])
+    around, sizes_late, writer_late = lax.optimization_barrier((gather_y(down_here), file_sizes, file_writer))
     place, lists, meta, most = route(
-        file_sizes, file_writer, tensors, lax.axis_index("expert"), lax.axis_index("row") & 1
+        file_sizes, file_writer, sizes_late, writer_late, tensors, lax.axis_index("expert"), lax.axis_index("row") & 1
     )
     which = jnp.sum(most > jnp.array(CAPACITIES[:-1], jnp.int32)).astype(jnp.int32)
-    down = gather(down_here, lax.axis_index("row"))
+    down = gather_core(around, lax.axis_index("row"))
     branches = [lambda *a, c=c: to_lines(c, *a) for c in CAPACITIES]
     groups = lax.switch(which, branches, place, lists, base, up, down)
     far, right, left = (send(groups[r], False, r) for r in (2, 1, 3))

time: 151 us -> 171 us (1.13); the launches traced: 150 us -> 173 us
  waiting for transfers between devices: 100 us -> 124 us
    ppermute x6, waiting for transfers between devices: 99.1 us -> 118 us  [send(): return lax.ppermute(block, ('expert', 'row'), pairs)]
    ppermute x7, waiting for transfers between devices: 1.34 us -> 6.07 us  [the longest x3 5.59 us: gather_y(): around[k] = lax.ppermute(down_here, 'row', pairs)]
  transfers between devices with their start and end apart: 13 -> 13, of which waited for: 6 -> 9; matrix products, arithmetic and copies ran while one was open for 6% -> 5% of each run, Pallas kernels for 5% -> 4%
where the time goes in v2:
time: 171 us; the launch traced here: 173 us
  waiting for transfers between devices  124 us (73%)
  Pallas kernels  19.9 us (12%)
  starting transfers between devices  18 us (11%)
  other arithmetic  7.49 us (4%)
  between operations  2.25 us (1%)
    ppermute x6, waiting for transfers between devices, send(): return lax.ppermute(block, ('expert', 'row'), pairs)  118 us
    ppermute x6, starting transfers between devices, send(): return lax.ppermute(block, ('expert', 'row'), pairs)  12.3 us
    pallas_call x2, Pallas kernels, unpack(): pl.pallas_call(kernel, out_shape=jax.ShapeDtypeStruct((slots, rows, width...  8.52 us
    pallas_call x1, Pallas kernels, merge(): pl.pallas_call(kernel, out_shape=jax.ShapeDtypeStruct((SIDE * capacity, r...  6.08 us
    ppermute x3, waiting for transfers between devices, gather_y(): around[k] = lax.ppermute(down_here, 'row', pairs)  5.59 us
    pallas_call x2, Pallas kernels, regroup(): pl.pallas_call(kernel, out_shape=[jax.ShapeDtypeStruct((SIDE, CAP, rows,...  5.27 us
    ppermute x3, starting transfers between devices, gather_y(): around[k] = lax.ppermute(down_here, 'row', pairs)  4.7 us
  transfers between devices with their start and end apart: 13, of which 9 were waited for; matrix products, arithmetic and copies ran while one was open for 5% of the time, Pallas kernels for 4%

profile of v2, /device:TPU:0, one launch (start us, length us, event | category | flops | bytes accessed | tf_op | source)
XLA Modules:
  0.0 173.1 jit_solution(6257032231648930623)
XLA Ops:
  0.0 0.0 copy-start
  0.0 3.1 %collective-permute-start.41 = (bf16[64,8,256]{2,1,0:T(8,128)(2,1)}, bf16[64,8,256]{2,1,0:T(8,128)(2,1)S(1)}, u32[]{:S(2)}, u32[]{:S(2)}) collective-permute-start(bf16[64,8,256]{2,1,0:T(8,128)(2,1)} %bitcast.77), channel_id=1, source_target_pairs={{0,6},{1,7},{2,0},{3,1},{4,2},{5,3},{6,4},{7,5},{8,14},{9,15},{10,... | collective-permute-start | bytes 786440 | tf_op jit(solution)/shard_map/ppermute | solution.py:125
  3.1 0.6 collective-permute-start.40
  3.7 1.0 collective-permute-start.39
  4.7 0.7 fusion.13
  5.4 0.7 fusion.10
  6.0 0.8 select_reduce_fusion.1
  6.8 0.8 select_reduce_fusion.2
  7.7 0.7 add_reduce_fusion
  9.7 0.1 select_reduce_fusion.5
  9.8 1.3 fusion.15
  11.8 0.1 pad_add_fusion.2
  11.9 0.7 fusion.5
  12.6 2.0 %collective-permute-done.41 = bf16[64,8,256]{2,1,0:T(8,128)(2,1)S(1)} collective-permute-done((bf16[64,8,256]{2,1,0:T(8,128)(2,1)}, bf16[64,8,256]{2,1,0:T(8,128)(2,1)S(1)}, u32[]{:S(2)}, u32[]{:S(2)}) %collective-permute-start.41) | collective-permute-done | bytes 262176 | tf_op jit(solution)/shard_map/ppermute | solution.py:125
  14.6 0.0 collective-permute-done.40
  14.6 3.6 %collective-permute-done.39 = bf16[64,8,256]{2,1,0:T(8,128)(2,1)S(1)} collective-permute-done((bf16[64,8,256]{2,1,0:T(8,128)(2,1)}, bf16[64,8,256]{2,1,0:T(8,128)(2,1)S(1)}, u32[]{:S(2)}, u32[]{:S(2)}) %collective-permute-start.39) | collective-permute-done | bytes 262176 | tf_op jit(solution)/shard_map/ppermute | solution.py:125
  18.2 0.0 collective-permute-start.42
  18.2 0.5 collective-permute-start.43
  18.7 0.0 collective-permute-start.44
  18.7 0.5 collective-permute-start.45
  19.2 0.7 fusion.30
  19.9 0.1 select_reduce_fusion
  20.0 0.1 pad_add_fusion.1
  20.1 0.2 broadcast_in_dim.124
  20.4 0.0 collective-permute-done.42
  20.4 0.0 collective-permute-done.43
  20.5 0.3 collective-permute-done.44
  20.9 0.0 copy-done
  20.9 0.1 collective-permute-done.45
  21.1 75.4 %conditional.1 = ((bf16[4,8,192,256]{3,2,1,0:T(8,128)(2,1)}, bf16[4,8,192,256]{3,2,1,0:T(8,128)(2,1)}, bf16[4,8,192,256]{3,2,1,0:T(8,128)(2,1)}, bf16[4,8,192,256]{3,2,1,0:T(8,128)(2,1)})) conditional(s32[]{:T(128)} %clamp.3, (s32[128]{0:T(128)S(1)}, bf16[64,192,256]{2,1,0:T(8,128)(2,1)}, ...), branch_computations={%region_13.14_spmd, %region_14.15_spmd, %region_15.16_spmd, %regio... | conditional | bytes 69206144 | solution.py:269
  21.4 6.1 %merge.23.refs_1_ = bf16[112,192,256]{2,1,0:T(8,128)(2,1)S(1)} custom-call(s32[128]{0:T(128)S(1)} %get-tuple-element.226.refs_0_, bf16[64,192,256]{2,1,0:T(8,128)(2,1)} %get-tuple-element.227.refs_1_, bf16[64,64,192]{2,1,0:T(8,128)(2,1)} %get-tuple-element.228.refs_2_, bf16[64,64,256]{2,1,0:T(8,128)(2,1)S(1)} %get-tuple-element.229.refs_3_), custom_call_target="tpu_custom_call" | custom-call | tf_op jit(solution)/shard_map/cond/branch_10_fun/merge/pallas_call | solution.py:102
  27.5 0.8 fusion.27
  28.3 4.0 %collective-permute-start.32 = (bf16[28,192,256]{2,1,0:T(8,128)(2,1)S(1)}, bf16[28,192,256]{2,1,0:T(8,128)(2,1)S(1)}, u32[]{:S(2)}, u32[]{:S(2)}) collective-permute-start(bf16[28,192,256]{2,1,0:T(8,128)(2,1)S(1)} %get-tuple-element.313), channel_id=1, source_target_pairs={{0,64},{32,96},{64,0},{96,32},{8,72},{40,104},{72,8},{104,40},{16,... | collective-permute-start | bytes 8257544 | tf_op jit(solution)/shard_map/cond/branch_10_fun/ppermute | solution.py:31
  32.3 0.7 collective-permute-start.31
  33.0 1.3 collective-permute-start.30
  34.3 29.1 %collective-permute-done.32.refs_2_ = bf16[28,192,256]{2,1,0:T(8,128)(2,1)S(1)} collective-permute-done((bf16[28,192,256]{2,1,0:T(8,128)(2,1)S(1)}, bf16[28,192,256]{2,1,0:T(8,128)(2,1)S(1)}, u32[]{:S(2)}, u32[]{:S(2)}) %collective-permute-start.32) | collective-permute-done | bytes 2752544 | tf_op jit(solution)/shard_map/cond/branch_10_fun/ppermute | solution.py:31
  63.4 2.6 %regroup.46 = (bf16[4,8,192,256]{3,2,1,0:T(8,128)(2,1)}, bf16[4,8,192,256]{3,2,1,0:T(8,128)(2,1)}, bf16[4,8,192,256]{3,2,1,0:T(8,128)(2,1)}, bf16[4,8,192,256]{3,2,1,0:T(8,128)(2,1)}) custom-call(s32[8]{0:T(128)S(1)} %get-tuple-element.225.refs_0_, bf16[112,192,256]{2,1,0:T(8,128)(2,1)S(1)} %merge.23.refs_1_, ...), custom_call_target="tpu_custom_call" | custom-call | bytes 6291456 | tf_op jit(solution)/shard_map/cond/branch_10_fun/regroup/pallas_call | solution.py:170
  66.0 27.8 %collective-permute-done.31.refs_2_ = bf16[28,192,256]{2,1,0:T(8,128)(2,1)S(1)} collective-permute-done((bf16[28,192,256]{2,1,0:T(8,128)(2,1)S(1)}, bf16[28,192,256]{2,1,0:T(8,128)(2,1)S(1)}, u32[]{:S(2)}, u32[]{:S(2)}) %collective-permute-start.31) | collective-permute-done | bytes 2752544 | tf_op jit(solution)/shard_map/cond/branch_10_fun/ppermute | solution.py:31
  93.8 0.0 collective-permute-done.30.refs_1_
  93.8 2.6 %regroup.47 = (bf16[4,8,192,256]{3,2,1,0:T(8,128)(2,1)}, bf16[4,8,192,256]{3,2,1,0:T(8,128)(2,1)}, bf16[4,8,192,256]{3,2,1,0:T(8,128)(2,1)}, bf16[4,8,192,256]{3,2,1,0:T(8,128)(2,1)}) custom-call(s32[8]{0:T(128)S(1)} %get-tuple-element.225.refs_0_, ...), custom_call_target="tpu_custom_call", output_to_operand_aliasing={{0}: (3, {}), {1}: (4, {}), {2}: (5, {}), {3}: (6, {})} | custom-call | bytes 6291456 | tf_op jit(solution)/shard_map/cond/branch_10_fun/regroup/pallas_call | solution.py:170
  96.5 3.1 %collective-permute-start.48 = (bf16[4,8,192,256]{3,2,1,0:T(8,128)(2,1)}, bf16[4,8,192,256]{3,2,1,0:T(8,128)(2,1)S(1)}, u32[]{:S(2)}, u32[]{:S(2)}) collective-permute-start(bf16[4,8,192,256]{3,2,1,0:T(8,128)(2,1)} %get-tuple-element.271), channel_id=1, source_target_pairs={{0,16},{8,24},{16,0},{24,8},{32,48},{40,56},{48,32},{56,40},{64,80... | collective-permute-start | bytes 9437192 | tf_op jit(solution)/shard_map/ppermute | solution.py:31
  99.6 0.6 collective-permute-start.46
  100.2 2.7 %collective-permute-start.47 = (bf16[4,8,192,256]{3,2,1,0:T(8,128)(2,1)}, bf16[4,8,192,256]{3,2,1,0:T(8,128)(2,1)S(1)}, u32[]{:S(2)}, u32[]{:S(2)}) collective-permute-start(bf16[4,8,192,256]{3,2,1,0:T(8,128)(2,1)} %get-tuple-element.269), channel_id=1, source_target_pairs={{0,24},{8,0},{16,8},{24,16},{32,56},{40,32},{48,40},{56,48},{64,88... | collective-permute-start | bytes 9437192 | tf_op jit(solution)/shard_map/ppermute | solution.py:31
  102.8 0.7 pad_add_fusion.refs_0_
  103.5 32.2 %collective-permute-done.48.refs_2_ = bf16[4,8,192,256]{3,2,1,0:T(8,128)(2,1)S(1)} collective-permute-done((bf16[4,8,192,256]{3,2,1,0:T(8,128)(2,1)}, bf16[4,8,192,256]{3,2,1,0:T(8,128)(2,1)S(1)}, u32[]{:S(2)}, u32[]{:S(2)}) %collective-permute-start.48) | collective-permute-done | bytes 3145760 | tf_op jit(solution)/shard_map/ppermute | solution.py:31
  135.7 4.9 %unpack.2.refs_3_ = bf16[8,192,4096]{2,1,0:T(8,128)(2,1)} custom-call(s32[4]{0:T(128)S(1)} %pad_add_fusion.refs_0_, bf16[4,8,192,256]{3,2,1,0:T(8,128)(2,1)} %get-tuple-element.270.refs_1_, bf16[4,8,192,256]{3,2,1,0:T(8,128)(2,1)S(1)} %collective-permute-done.48.refs_2_), custom_call_target="tpu_custom_call" | custom-call | bytes 12582912 | tf_op jit(solution)/shard_map/unpack/pallas_call | solution.py:227
  140.6 28.7 %collective-permute-done.46.refs_1_ = bf16[4,8,192,256]{3,2,1,0:T(8,128)(2,1)S(1)} collective-permute-done((bf16[4,8,192,256]{3,2,1,0:T(8,128)(2,1)}, bf16[4,8,192,256]{3,2,1,0:T(8,128)(2,1)S(1)}, u32[]{:S(2)}, u32[]{:S(2)}) %collective-permute-start.46) | collective-permute-done | bytes 3145760 | tf_op jit(solution)/shard_map/ppermute | solution.py:31
  169.3 0.1 collective-permute-done.47.refs_2_
  169.4 3.6 %unpack.3 = bf16[8,192,4096]{2,1,0:T(8,128)(2,1)} custom-call(s32[4]{0:T(128)S(1)} %pad_add_fusion.refs_0_, bf16[4,8,192,256]{3,2,1,0:T(8,128)(2,1)S(1)} %collective-permute-done.46.refs_1_, bf16[4,8,192,256]{3,2,1,0:T(8,128)(2,1)S(1)} %collective-permute-done.47.refs_2_, bf16[8,192,4096]{2,1,0:T(8,128)(2,1)} %unpack.2.refs_3_), custom_call_target="tpu_custom_call", output_to_operand_aliasing={{}: (3, {})} | custom-call | bytes 12582912 | tf_op jit(solution)/shard_map/unpack/pallas_call | solution.py:227
  (8 shorter events, 0.2 us)
Async XLA Ops:
  0.0 20.9 %copy-start = (bf16[32,2,8,256]{3,2,1,0:T(8,128)(2,1)S(1)}, bf16[32,2,8,256]{3,2,1,0:T(8,128)(2,1)}, u32[]{:S(2)}) copy-start(bf16[32,2,8,256]{3,2,1,0:T(8,128)(2,1)} %param.30) | copy-start | bytes 786436
  0.0 14.6 %collective-permute-start.41 = (bf16[64,8,256]{2,1,0:T(8,128)(2,1)}, bf16[64,8,256]{2,1,0:T(8,128)(2,1)S(1)}, u32[]{:S(2)}, u32[]{:S(2)}) collective-permute-start(bf16[64,8,256]{2,1,0:T(8,128)(2,1)} %bitcast.77), channel_id=1, source_target_pairs={{0,6},{1,7},{2,0},{3,1},{4,2},{5,3},{6,4},{7,5},{8,14},{9,15},{10,... | collective-permute-start | bytes 786440 | tf_op jit(solution)/shard_map/ppermute | solution.py:125
  3.1 11.5 %collective-permute-start.40 = (bf16[64,8,256]{2,1,0:T(8,128)(2,1)}, bf16[64,8,256]{2,1,0:T(8,128)(2,1)S(1)}, u32[]{:S(2)}, u32[]{:S(2)}) collective-permute-start(bf16[64,8,256]{2,1,0:T(8,128)(2,1)} %bitcast.78), channel_id=1, source_target_pairs={{0,4},{1,5},{2,6},{3,7},{4,0},{5,1},{6,2},{7,3},{8,12},{9,13},{10,... | collective-permute-start | bytes 786440 | tf_op jit(solution)/shard_map/ppermute | solution.py:125
  3.7 14.5 %collective-permute-start.39 = (bf16[64,8,256]{2,1,0:T(8,128)(2,1)}, bf16[64,8,256]{2,1,0:T(8,128)(2,1)S(1)}, u32[]{:S(2)}, u32[]{:S(2)}) collective-permute-start(bf16[64,8,256]{2,1,0:T(8,128)(2,1)} %bitcast.79), channel_id=1, source_target_pairs={{0,2},{1,3},{2,4},{3,5},{4,6},{5,7},{6,0},{7,1},{8,10},{9,11},{10,... | collective-permute-start | bytes 786440 | tf_op jit(solution)/shard_map/ppermute | solution.py:125
  18.2 2.2 %collective-permute-start.42 = (bf16[64,8,256]{2,1,0:T(8,128)(2,1)S(1)}, bf16[64,8,256]{2,1,0:T(8,128)(2,1)S(1)}, u32[]{:S(2)}, u32[]{:S(2)}) collective-permute-start(bf16[64,8,256]{2,1,0:T(8,128)(2,1)S(1)} %collective-permute-done.39), channel_id=1, source_target_pairs={{0,1},{1,0},{2,3},{3,2},{4,5},{5,4},{6,7},{7,6},{8,9},{9,8},{10,11... | collective-permute-start | bytes 786440 | tf_op jit(solution)/shard_map/ppermute | solution.py:139
  18.2 2.2 %collective-permute-start.43 = (bf16[64,8,256]{2,1,0:T(8,128)(2,1)S(1)}, bf16[64,8,256]{2,1,0:T(8,128)(2,1)S(1)}, u32[]{:S(2)}, u32[]{:S(2)}) collective-permute-start(bf16[64,8,256]{2,1,0:T(8,128)(2,1)S(1)} %collective-permute-done.41), channel_id=1, source_target_pairs={{0,1},{1,0},{2,3},{3,2},{4,5},{5,4},{6,7},{7,6},{8,9},{9,8},{10,11... | collective-permute-start | bytes 786440 | tf_op jit(solution)/shard_map/ppermute | solution.py:139
  18.7 2.1 %collective-permute-start.44 = (bf16[64,8,256]{2,1,0:T(8,128)(2,1)S(1)}, bf16[64,8,256]{2,1,0:T(8,128)(2,1)S(1)}, u32[]{:S(2)}, u32[]{:S(2)}) collective-permute-start(bf16[64,8,256]{2,1,0:T(8,128)(2,1)S(1)} %collective-permute-done.40), channel_id=1, source_target_pairs={{0,1},{1,0},{2,3},{3,2},{4,5},{5,4},{6,7},{7,6},{8,9},{9,8},{10,11... | collective-permute-start | bytes 786440 | tf_op jit(solution)/shard_map/ppermute | solution.py:139
  18.7 2.3 %collective-permute-start.45 = (bf16[64,8,256]{2,1,0:T(8,128)(2,1)}, bf16[64,8,256]{2,1,0:T(8,128)(2,1)S(1)}, u32[]{:S(2)}, u32[]{:S(2)}) collective-permute-start(bf16[64,8,256]{2,1,0:T(8,128)(2,1)} %bitcast.80), channel_id=1, source_target_pairs={{0,1},{1,0},{2,3},{3,2},{4,5},{5,4},{6,7},{7,6},{8,9},{9,8},{10,11... | collective-permute-start | bytes 786440 | tf_op jit(solution)/shard_map/ppermute | solution.py:139
  28.3 35.1 %collective-permute-start.32 = (bf16[28,192,256]{2,1,0:T(8,128)(2,1)S(1)}, bf16[28,192,256]{2,1,0:T(8,128)(2,1)S(1)}, u32[]{:S(2)}, u32[]{:S(2)}) collective-permute-start(bf16[28,192,256]{2,1,0:T(8,128)(2,1)S(1)} %get-tuple-element.313), channel_id=1, source_target_pairs={{0,64},{32,96},{64,0},{96,32},{8,72},{40,104},{72,8},{104,40},{16,... | collective-permute-start | bytes 8257544 | tf_op jit(solution)/shard_map/cond/branch_10_fun/ppermute | solution.py:31
  32.3 61.6 %collective-permute-start.31 = (bf16[28,192,256]{2,1,0:T(8,128)(2,1)S(1)}, bf16[28,192,256]{2,1,0:T(8,128)(2,1)S(1)}, u32[]{:S(2)}, u32[]{:S(2)}) collective-permute-start(bf16[28,192,256]{2,1,0:T(8,128)(2,1)S(1)} %get-tuple-element.314), channel_id=1, source_target_pairs={{0,96},{32,0},{64,32},{96,64},{8,104},{40,8},{72,40},{104,72},{16,... | collective-permute-start | bytes 8257544 | tf_op jit(solution)/shard_map/cond/branch_10_fun/ppermute | solution.py:31
  33.0 60.9 %collective-permute-start.30 = (bf16[28,192,256]{2,1,0:T(8,128)(2,1)S(1)}, bf16[28,192,256]{2,1,0:T(8,128)(2,1)S(1)}, u32[]{:S(2)}, u32[]{:S(2)}) collective-permute-start(bf16[28,192,256]{2,1,0:T(8,128)(2,1)S(1)} %get-tuple-element.315), channel_id=1, source_target_pairs={{0,32},{32,64},{64,96},{96,0},{8,40},{40,72},{72,104},{104,8},{16,... | collective-permute-start | bytes 8257544 | tf_op jit(solution)/shard_map/cond/branch_10_fun/ppermute | solution.py:31
  96.5 39.2 %collective-permute-start.48 = (bf16[4,8,192,256]{3,2,1,0:T(8,128)(2,1)}, bf16[4,8,192,256]{3,2,1,0:T(8,128)(2,1)S(1)}, u32[]{:S(2)}, u32[]{:S(2)}) collective-permute-start(bf16[4,8,192,256]{3,2,1,0:T(8,128)(2,1)} %get-tuple-element.271), channel_id=1, source_target_pairs={{0,16},{8,24},{16,0},{24,8},{32,48},{40,56},{48,32},{56,40},{64,80... | collective-permute-start | bytes 9437192 | tf_op jit(solution)/shard_map/ppermute | solution.py:31
  99.6 69.7 %collective-permute-start.46 = (bf16[4,8,192,256]{3,2,1,0:T(8,128)(2,1)}, bf16[4,8,192,256]{3,2,1,0:T(8,128)(2,1)S(1)}, u32[]{:S(2)}, u32[]{:S(2)}) collective-permute-start(bf16[4,8,192,256]{3,2,1,0:T(8,128)(2,1)} %get-tuple-element.268), channel_id=1, source_target_pairs={{0,8},{8,16},{16,24},{24,0},{32,40},{40,48},{48,56},{56,32},{64,72... | collective-permute-start | bytes 9437192 | tf_op jit(solution)/shard_map/ppermute | solution.py:31
  100.2 69.2 %collective-permute-start.47 = (bf16[4,8,192,256]{3,2,1,0:T(8,128)(2,1)}, bf16[4,8,192,256]{3,2,1,0:T(8,128)(2,1)S(1)}, u32[]{:S(2)}, u32[]{:S(2)}) collective-permute-start(bf16[4,8,192,256]{3,2,1,0:T(8,128)(2,1)} %get-tuple-element.269), channel_id=1, source_target_pairs={{0,24},{8,0},{16,8},{24,16},{32,56},{40,32},{48,40},{56,48},{64,88... | collective-permute-start | bytes 9437192 | tf_op jit(solution)/shard_map/ppermute | solution.py:31
